TPU v7x, 256 devices: a whole 4x4x8 slice. The times are simulated.
256 devices in a mesh: slab: 64 (over z, x, core), energy: 4 (over y).
Axes of the slice: x: 4, y: 4, z: 8, core: 2. Of those that a mesh axis runs over, the one named last changes fastest.
Arguments:
- energy_sq: float32 [4], P('energy'), may hold values from 2.5 to 3.3
- broadening: float32 [4], P('energy'), may hold values from 0.05 to 0.1
- onsite: float32 [64, 192, 192], P('slab'), may hold values from -0.005051815 to 2
- coupling: float32 [64, 192, 192], P('slab'), may hold values from -0.005051815 to 0.005051815
- sigma_in: float32 [4, 64, 192, 384], P('energy', 'slab'), may hold values from -0.02 to 0.005051815
- anharmonic: float32 [64, 192, 192], P('slab'), may hold values from 0.5 to 2
- energy_pairs: int32 [4, 8, 2], P('energy'), may hold values from 0 to 3
Outputs:
- green_diag: float32 [4, 64, 192, 384], P('energy', 'slab')
- sigma_out: float32 [4, 64, 192, 384], P('energy', 'slab')
All inputs are finite; a program needn't handle non-finite values.
Results may differ from a plain program's by a relative error of at most 0.0003.
Values sent between devices are 32-bit elements; how exact they have to be, the bound alone decides.
A program may use at most 128 MiB of HBM per device.

v0:
```python
import jax
import jax.numpy as jnp
from jax import lax
from jax.sharding import PartitionSpec as P


def shifted(value, axis, steps):
    count = lax.axis_size(axis)
    first, last = (max(0, -steps), min(count, count - steps))
    return lax.ppermute(value, axis, [(source, source + steps) for source in range(first, last)])


def complex_product(left, right):
    block_width = left.shape[-2]
    high = lax.Precision.HIGHEST
    right_real = right[..., :block_width]
    right_imag = right[..., block_width:]
    stacked = jnp.concatenate(
        [
            jnp.concatenate([right_real, right_imag], -1),
            jnp.concatenate([-right_imag, right_real], -1),
        ],
        -2,
    )
    return jnp.einsum("...ij,...jk->...ik", left, stacked, precision=high)


def invert(matrix):
    block_width = matrix.shape[-2]
    high = lax.Precision.HIGHEST
    real_part = matrix[..., :block_width]
    imag_part = matrix[..., block_width:]
    real_part = 0.5 * (real_part + jnp.swapaxes(real_part, -1, -2))
    imag_part = 0.5 * (imag_part + jnp.swapaxes(imag_part, -1, -2))
    identity = jnp.broadcast_to(jnp.eye(block_width, dtype=jnp.float32), real_part.shape)
    imag_factor = jnp.linalg.cholesky(imag_part)
    factor_inverse = jax.scipy.linalg.solve_triangular(imag_factor, identity, lower=True)
    factor_trans = jnp.swapaxes(factor_inverse, -1, -2)
    middle = jnp.einsum(
        "...ij,...jk,...kl->...il", factor_inverse, real_part, factor_trans, precision=high
    )
    middle = 0.5 * (middle + jnp.swapaxes(middle, -1, -2))
    squared = jnp.einsum("...ij,...jk->...ik", middle, middle, precision=high) + identity
    square_factor = jnp.linalg.cholesky(squared)
    right_side = jax.scipy.linalg.cho_solve((square_factor, True), factor_inverse)
    first_real = jnp.einsum(
        "...ij,...jk,...kl->...il", factor_trans, middle, right_side, precision=high
    )
    first_imag = -jnp.einsum("...ij,...jk->...ik", factor_trans, right_side, precision=high)
    first = jnp.concatenate([first_real, first_imag], -1)
    first = 2.0 * first - complex_product(first, complex_product(matrix, first))
    return first


def reduce_levels(matrix, lower_block, upper_block):
    slab_count = lax.axis_size("slab")
    level_count = slab_count.bit_length() - 1
    for level_index in range(level_count):
        distance = 2**level_index
        inverse = invert(matrix)
        forward = complex_product(inverse, upper_block)
        backward = complex_product(inverse, lower_block)
        if level_index + 1 < level_count:
            payload = jnp.stack([forward, backward])
            low_side = shifted(payload, "slab", distance)
            high_side = shifted(payload, "slab", -distance)
            matrix = (
                matrix
                - complex_product(lower_block, low_side[0])
                - complex_product(upper_block, high_side[1])
            )
            new_lower = -complex_product(lower_block, low_side[1])
            new_upper = -complex_product(upper_block, high_side[0])
            lower_block = new_lower
            upper_block = new_upper
        else:
            last_payload = jnp.stack([forward, backward])
            low_pair = shifted(last_payload, "slab", distance)
            high_pair = shifted(last_payload, "slab", -distance)
            low_forward = low_pair[0]
            high_backward = high_pair[1]
            matrix = (
                matrix
                - complex_product(lower_block, low_forward)
                - complex_product(upper_block, high_backward)
            )
    return invert(matrix)


def shards(energy_sq, broadening, onsite, coupling, sigma_in, anharmonic, energy_pairs):
    block_width = onsite.shape[-1]
    energy_count = energy_sq.shape[0]
    identity = jnp.eye(block_width, dtype=jnp.float32)
    blank = jnp.zeros((block_width, block_width), jnp.float32)
    bond_block = identity + coupling[0]
    bond_below = shifted(bond_block, "slab", 1)
    upper_one = jnp.concatenate([-bond_block, blank], -1)
    lower_one = jnp.concatenate([-bond_below.T, blank], -1)
    self_part = sigma_in[:, 0]
    diag_real = (
        energy_sq[:, None, None] * identity[None] - onsite[0][None] - self_part[..., :block_width]
    )
    diag_imag = broadening[:, None, None] * identity[None] - self_part[..., block_width:]
    matrix = jnp.concatenate([diag_real, diag_imag], -1)
    upper_all = jnp.broadcast_to(upper_one, (energy_count, block_width, 2 * block_width))
    lower_all = jnp.broadcast_to(lower_one, (energy_count, block_width, 2 * block_width))
    green_local = reduce_levels(matrix, lower_all, upper_all)
    everyone = lax.all_gather(green_local[:, None], "energy", axis=0, tiled=True)[:, 0]
    pair_count = energy_pairs.shape[1]
    first = jnp.take(everyone, energy_pairs[:, :, 0], axis=0)
    second = jnp.take(everyone, energy_pairs[:, :, 1], axis=0)
    real_part = (
        first[..., :block_width] * second[..., :block_width]
        - first[..., block_width:] * second[..., block_width:]
    )
    imag_part = (
        first[..., :block_width] * second[..., block_width:]
        + first[..., block_width:] * second[..., :block_width]
    )
    summed_real = jnp.sum(real_part, axis=1)
    summed_imag = jnp.sum(imag_part, axis=1)
    scale = anharmonic[0] / pair_count
    sigma_local = jnp.concatenate([summed_real * scale[None], summed_imag * scale[None]], -1)
    return (green_local[:, None], sigma_local[:, None])


def solution(mesh):
    in_specs = (
        P("energy"),
        P("energy"),
        P("slab", None, None),
        P("slab", None, None),
        P("energy", "slab", None, None),
        P("slab", None, None),
        P("energy", None, None),
    )
    out_specs = (P("energy", "slab", None, None), P("energy", "slab", None, None))
    return jax.shard_map(shards, mesh=mesh, in_specs=in_specs, out_specs=out_specs, check_vma=False)
```

profile of v0, /device:TPU:32, one launch (start us, length us, event | category | flops | bytes accessed | tf_op | source)
XLA Modules:
  0.0 1012.8 jit_solution(17196710646150836668)
XLA Ops:
  13.4 11.7 %custom-call.81 = f32[1,128,128]{2,1,0:T(8,128)S(1)} custom-call(f32[1,128,128]{2,1,0:T(8,128)S(1)} %copy.15), custom_call_target="Cholesky" | custom-call | tf_op jit(solution)/shard_map/jit(cholesky)/cholesky | solution.py:36
  25.7 9.8 custom-call.82
  36.1 5.9 custom-call.83
  44.1 19.9 %custom-call.84 = f32[2,128,128]{1,2,0:T(8,128)S(1)} custom-call(f32[2,128,128]{2,1,0:T(8,128)S(1)} %pad_maximum_fusion.34), custom_call_target="InvertDiagBlocksLowerTriangular" | custom-call | tf_op jit(solution)/shard_map/jit(_solve_triangular)/triangular_solve/custom-call.1 | solution.py:37
  66.9 11.7 %custom-call.85 = f32[1,128,128]{2,1,0:T(8,128)S(1)} custom-call(f32[1,128,128]{2,1,0:T(8,128)S(1)} %cholesky.1192), custom_call_target="Cholesky" | custom-call | tf_op jit(solution)/shard_map/jit(cholesky)/cholesky | solution.py:44
  79.3 9.8 custom-call.86
  89.5 5.8 custom-call.87
  97.5 20.1 %custom-call.88 = f32[2,128,128]{1,2,0:T(8,128)S(1)} custom-call(f32[2,128,128]{2,1,0:T(8,128)S(1)} %pad_maximum_fusion.35), custom_call_target="InvertDiagBlocksLowerTriangular" | custom-call | tf_op jit(solution)/shard_map/jit(_cho_solve)/triangular_solve | solution.py:45
  145.6 11.7 %custom-call.90 = f32[1,128,128]{2,1,0:T(8,128)S(1)} custom-call(f32[1,128,128]{2,1,0:T(8,128)S(1)} %copy.29), custom_call_target="Cholesky" | custom-call | tf_op jit(solution)/shard_map/jit(cholesky)/cholesky | solution.py:36
  158.0 9.8 custom-call.91
  168.4 5.9 custom-call.92
  176.5 19.9 %custom-call.93 = f32[2,128,128]{1,2,0:T(8,128)S(1)} custom-call(f32[2,128,128]{2,1,0:T(8,128)S(1)} %pad_maximum_fusion.36), custom_call_target="InvertDiagBlocksLowerTriangular" | custom-call | tf_op jit(solution)/shard_map/jit(_solve_triangular)/triangular_solve/custom-call.1 | solution.py:37
  199.3 11.7 %custom-call.94 = f32[1,128,128]{2,1,0:T(8,128)S(1)} custom-call(f32[1,128,128]{2,1,0:T(8,128)S(1)} %cholesky.1198), custom_call_target="Cholesky" | custom-call | tf_op jit(solution)/shard_map/jit(cholesky)/cholesky | solution.py:44
  211.7 9.8 custom-call.95
  221.9 5.8 custom-call.96
  229.9 20.1 %custom-call.97 = f32[2,128,128]{1,2,0:T(8,128)S(1)} custom-call(f32[2,128,128]{2,1,0:T(8,128)S(1)} %pad_maximum_fusion.37), custom_call_target="InvertDiagBlocksLowerTriangular" | custom-call | tf_op jit(solution)/shard_map/jit(_cho_solve)/triangular_solve | solution.py:45
  264.3 8.3 collective-permute-done.4
  272.8 6.1 collective-permute-done.3
  281.2 11.7 %custom-call.99 = f32[1,128,128]{2,1,0:T(8,128)S(1)} custom-call(f32[1,128,128]{2,1,0:T(8,128)S(1)} %copy.43), custom_call_target="Cholesky" | custom-call | tf_op jit(solution)/shard_map/jit(cholesky)/cholesky | solution.py:36
  293.6 9.8 custom-call.100
  304.0 5.9 custom-call.101
  312.1 19.9 %custom-call.102 = f32[2,128,128]{1,2,0:T(8,128)S(1)} custom-call(f32[2,128,128]{2,1,0:T(8,128)S(1)} %pad_maximum_fusion.38), custom_call_target="InvertDiagBlocksLowerTriangular" | custom-call | tf_op jit(solution)/shard_map/jit(_solve_triangular)/triangular_solve/custom-call.1 | solution.py:37
  334.9 11.7 %custom-call.103 = f32[1,128,128]{2,1,0:T(8,128)S(1)} custom-call(f32[1,128,128]{2,1,0:T(8,128)S(1)} %cholesky.1204), custom_call_target="Cholesky" | custom-call | tf_op jit(solution)/shard_map/jit(cholesky)/cholesky | solution.py:44
  347.3 9.8 custom-call.104
  357.5 5.8 custom-call.105
  365.5 20.1 %custom-call.106 = f32[2,128,128]{1,2,0:T(8,128)S(1)} custom-call(f32[2,128,128]{2,1,0:T(8,128)S(1)} %pad_maximum_fusion.39), custom_call_target="InvertDiagBlocksLowerTriangular" | custom-call | tf_op jit(solution)/shard_map/jit(_cho_solve)/triangular_solve | solution.py:45
  401.4 22.2 %collective-permute-done.6 = f32[2,1,192,384]{3,2,1,0:T(8,128)S(1)} collective-permute-done((f32[2,1,192,384]{3,2,1,0:T(8,128)S(1)}, f32[2,1,192,384]{3,2,1,0:T(8,128)S(1)}, u32[]{:S(2)}, u32[]{:S(2)}) %collective-permute-start.6) | collective-permute-done | bytes 589856 | tf_op jit(solution)/shard_map/ppermute | solution.py:10
  426.1 11.7 %custom-call.108 = f32[1,128,128]{2,1,0:T(8,128)S(1)} custom-call(f32[1,128,128]{2,1,0:T(8,128)S(1)} %copy.57), custom_call_target="Cholesky" | custom-call | tf_op jit(solution)/shard_map/jit(cholesky)/cholesky | solution.py:36
  438.5 9.8 custom-call.109
  448.9 5.9 custom-call.110
  457.0 19.9 %custom-call.111 = f32[2,128,128]{1,2,0:T(8,128)S(1)} custom-call(f32[2,128,128]{2,1,0:T(8,128)S(1)} %pad_maximum_fusion.40), custom_call_target="InvertDiagBlocksLowerTriangular" | custom-call | tf_op jit(solution)/shard_map/jit(_solve_triangular)/triangular_solve/custom-call.1 | solution.py:37
  479.8 11.7 %custom-call.112 = f32[1,128,128]{2,1,0:T(8,128)S(1)} custom-call(f32[1,128,128]{2,1,0:T(8,128)S(1)} %cholesky.1210), custom_call_target="Cholesky" | custom-call | tf_op jit(solution)/shard_map/jit(cholesky)/cholesky | solution.py:44
  492.2 9.8 custom-call.113
  502.4 5.8 custom-call.114
  510.4 20.1 %custom-call.115 = f32[2,128,128]{1,2,0:T(8,128)S(1)} custom-call(f32[2,128,128]{2,1,0:T(8,128)S(1)} %pad_maximum_fusion.41), custom_call_target="InvertDiagBlocksLowerTriangular" | custom-call | tf_op jit(solution)/shard_map/jit(_cho_solve)/triangular_solve | solution.py:45
  544.8 8.8 collective-permute-done.8
  557.7 11.7 %custom-call.117 = f32[1,128,128]{2,1,0:T(8,128)S(1)} custom-call(f32[1,128,128]{2,1,0:T(8,128)S(1)} %copy.71), custom_call_target="Cholesky" | custom-call | tf_op jit(solution)/shard_map/jit(cholesky)/cholesky | solution.py:36
  570.1 9.8 custom-call.118
  580.5 5.9 custom-call.119
  588.6 19.9 %custom-call.120 = f32[2,128,128]{1,2,0:T(8,128)S(1)} custom-call(f32[2,128,128]{2,1,0:T(8,128)S(1)} %pad_maximum_fusion.42), custom_call_target="InvertDiagBlocksLowerTriangular" | custom-call | tf_op jit(solution)/shard_map/jit(_solve_triangular)/triangular_solve/custom-call.1 | solution.py:37
  611.4 11.7 %custom-call.121 = f32[1,128,128]{2,1,0:T(8,128)S(1)} custom-call(f32[1,128,128]{2,1,0:T(8,128)S(1)} %cholesky.1216), custom_call_target="Cholesky" | custom-call | tf_op jit(solution)/shard_map/jit(cholesky)/cholesky | solution.py:44
  623.8 9.8 custom-call.122
  634.0 5.8 custom-call.123
  642.0 20.1 %custom-call.124 = f32[2,128,128]{1,2,0:T(8,128)S(1)} custom-call(f32[2,128,128]{2,1,0:T(8,128)S(1)} %pad_maximum_fusion.43), custom_call_target="InvertDiagBlocksLowerTriangular" | custom-call | tf_op jit(solution)/shard_map/jit(_cho_solve)/triangular_solve | solution.py:45
  671.6 10.3 %collective-permute-start.9 = (f32[2,1,192,384]{3,2,1,0:T(8,128)S(1)}, f32[2,1,192,384]{3,2,1,0:T(8,128)S(1)}, u32[]{:S(2)}, u32[]{:S(2)}) collective-permute-start(f32[2,1,192,384]{3,2,1,0:T(8,128)S(1)} %pad_maximum_fusion.4), channel_id=1, source_target_pairs={{0,64},{4,68},{8,72},{12,76},{16,80},{20,84},{24,88},{28,92},{32,9... | collective-permute-start | bytes 1769480 | tf_op jit(solution)/shard_map/ppermute | solution.py:10
  681.9 8.3 collective-permute-done.10
  690.3 11.4 %collective-permute-done.9 = f32[2,1,192,384]{3,2,1,0:T(8,128)S(1)} collective-permute-done((f32[2,1,192,384]{3,2,1,0:T(8,128)S(1)}, f32[2,1,192,384]{3,2,1,0:T(8,128)S(1)}, u32[]{:S(2)}, u32[]{:S(2)}) %collective-permute-start.9) | collective-permute-done | bytes 589856 | tf_op jit(solution)/shard_map/ppermute | solution.py:10
  704.0 11.7 %custom-call.126 = f32[1,128,128]{2,1,0:T(8,128)S(1)} custom-call(f32[1,128,128]{2,1,0:T(8,128)S(1)} %copy.85), custom_call_target="Cholesky" | custom-call | tf_op jit(solution)/shard_map/jit(cholesky)/cholesky | solution.py:36
  716.5 9.8 custom-call.127
  726.8 5.9 custom-call.128
  734.9 19.9 %custom-call.129 = f32[2,128,128]{1,2,0:T(8,128)S(1)} custom-call(f32[2,128,128]{2,1,0:T(8,128)S(1)} %pad_maximum_fusion.44), custom_call_target="InvertDiagBlocksLowerTriangular" | custom-call | tf_op jit(solution)/shard_map/jit(_solve_triangular)/triangular_solve/custom-call.1 | solution.py:37
  757.7 11.7 %custom-call.130 = f32[1,128,128]{2,1,0:T(8,128)S(1)} custom-call(f32[1,128,128]{2,1,0:T(8,128)S(1)} %cholesky.1222), custom_call_target="Cholesky" | custom-call | tf_op jit(solution)/shard_map/jit(cholesky)/cholesky | solution.py:44
  770.1 9.8 custom-call.131
  788.3 20.1 %custom-call.133 = f32[2,128,128]{1,2,0:T(8,128)S(1)} custom-call(f32[2,128,128]{2,1,0:T(8,128)S(1)} %pad_maximum_fusion.45), custom_call_target="InvertDiagBlocksLowerTriangular" | custom-call | tf_op jit(solution)/shard_map/jit(_cho_solve)/triangular_solve | solution.py:45
  818.0 8.7 collective-permute-start.11
  826.7 22.4 %collective-permute-done.12 = f32[2,1,192,384]{3,2,1,0:T(8,128)S(1)} collective-permute-done((f32[2,1,192,384]{3,2,1,0:T(8,128)S(1)}, f32[2,1,192,384]{3,2,1,0:T(8,128)S(1)}, u32[]{:S(2)}, u32[]{:S(2)}) %collective-permute-start.12) | collective-permute-done | bytes 589856 | tf_op jit(solution)/shard_map/ppermute | solution.py:10
  851.7 11.7 %custom-call.135 = f32[1,128,128]{2,1,0:T(8,128)S(1)} custom-call(f32[1,128,128]{2,1,0:T(8,128)S(1)} %cholesky.1225), custom_call_target="Cholesky" | custom-call | tf_op jit(solution)/shard_map/jit(cholesky)/cholesky | solution.py:36
  864.1 9.8 custom-call.136
  874.3 5.8 custom-call.137
  882.4 19.9 %custom-call.138 = f32[2,128,128]{1,2,0:T(8,128)S(1)} custom-call(f32[2,128,128]{2,1,0:T(8,128)S(1)} %pad_maximum_fusion.46), custom_call_target="InvertDiagBlocksLowerTriangular" | custom-call | tf_op jit(solution)/shard_map/jit(_solve_triangular)/triangular_solve/custom-call.1 | solution.py:37
  904.9 11.7 %custom-call.139 = f32[1,128,128]{2,1,0:T(8,128)S(1)} custom-call(f32[1,128,128]{2,1,0:T(8,128)S(1)} %cholesky.1228), custom_call_target="Cholesky" | custom-call | tf_op jit(solution)/shard_map/jit(cholesky)/cholesky | solution.py:44
  917.3 9.8 custom-call.140
  935.5 19.9 %custom-call.142 = f32[2,128,128]{1,2,0:T(8,128)S(1)} custom-call(f32[2,128,128]{2,1,0:T(8,128)S(1)} %pad_maximum_fusion.47), custom_call_target="InvertDiagBlocksLowerTriangular" | custom-call | tf_op jit(solution)/shard_map/jit(_cho_solve)/triangular_solve | solution.py:45
  960.7 36.6 %all-gather.3.cloned.1.call-done = f32[768,384]{1,0:T(8,128)} async-done(((f32[192,384]{1,0:T(8,128)}), f32[768,384]{1,0:T(8,128)}) %all-gather.3.cloned.1.call-update) | async-done | bytes 1179664 | tf_op jit(solution)/shard_map/all_gather | solution.py:108
  (529 shorter events, 181.1 us)
Async XLA Ops:
  7.2 990.2 %all-gather.3.cloned.1.call-start = ((), (), s32[]{:S(2)}) async-start(), calls=%async_computation | async-start | bytes 1474560 | tf_op jit(solution)/shard_map/all_gather | solution.py:108
  8.3 114.7 %collective-permute-start = (f32[192,192]{0,1:T(8,128)S(1)}, f32[192,192]{0,1:T(8,128)S(1)}, u32[]{:S(2)}, u32[]{:S(2)}) collective-permute-start(f32[192,192]{0,1:T(8,128)S(1)} %get-tuple-element.293), channel_id=1, source_target_pairs={{0,4},{4,8},{8,12},{12,16},{16,20},{20,24},{24,28},{28,32},{32,36}... | collective-permute-start | bytes 442376 | tf_op jit(solution)/shard_map/ppermute | solution.py:10
  124.1 13.1 %collective-permute-start.2 = (f32[2,1,192,384]{3,2,1,0:T(8,128)S(1)}, f32[2,1,192,384]{3,2,1,0:T(8,128)S(1)}, u32[]{:S(2)}, u32[]{:S(2)}) collective-permute-start(f32[2,1,192,384]{3,2,1,0:T(8,128)S(1)} %pad_maximum_fusion), channel_id=1, source_target_pairs={{4,0},{8,4},{12,8},{16,12},{20,16},{24,20},{28,24},{32,28},{36,32}... | collective-permute-start | bytes 1769480 | tf_op jit(solution)/shard_map/ppermute | solution.py:10
  129.8 13.3 %collective-permute-start.1 = (f32[2,1,192,384]{3,2,1,0:T(8,128)S(1)}, f32[2,1,192,384]{3,2,1,0:T(8,128)S(1)}, u32[]{:S(2)}, u32[]{:S(2)}) collective-permute-start(f32[2,1,192,384]{3,2,1,0:T(8,128)S(1)} %pad_maximum_fusion), channel_id=1, source_target_pairs={{0,4},{4,8},{8,12},{12,16},{16,20},{20,24},{24,28},{28,32},{32,36}... | collective-permute-start | bytes 1769480 | tf_op jit(solution)/shard_map/ppermute | solution.py:10
  258.3 14.3 %collective-permute-start.4 = (f32[2,1,192,384]{3,2,1,0:T(8,128)S(1)}, f32[2,1,192,384]{3,2,1,0:T(8,128)S(1)}, u32[]{:S(2)}, u32[]{:S(2)}) collective-permute-start(f32[2,1,192,384]{3,2,1,0:T(8,128)S(1)} %pad_maximum_fusion.1), channel_id=1, source_target_pairs={{8,0},{12,4},{16,8},{20,12},{24,16},{28,20},{32,24},{36,28},{40,32... | collective-permute-start | bytes 1769480 | tf_op jit(solution)/shard_map/ppermute | solution.py:10
  260.2 18.6 %collective-permute-start.3 = (f32[2,1,192,384]{3,2,1,0:T(8,128)S(1)}, f32[2,1,192,384]{3,2,1,0:T(8,128)S(1)}, u32[]{:S(2)}, u32[]{:S(2)}) collective-permute-start(f32[2,1,192,384]{3,2,1,0:T(8,128)S(1)} %pad_maximum_fusion.1), channel_id=1, source_target_pairs={{0,8},{4,12},{8,16},{12,20},{16,24},{20,28},{24,32},{28,36},{32,40... | collective-permute-start | bytes 1769480 | tf_op jit(solution)/shard_map/ppermute | solution.py:10
  393.8 29.7 %collective-permute-start.6 = (f32[2,1,192,384]{3,2,1,0:T(8,128)S(1)}, f32[2,1,192,384]{3,2,1,0:T(8,128)S(1)}, u32[]{:S(2)}, u32[]{:S(2)}) collective-permute-start(f32[2,1,192,384]{3,2,1,0:T(8,128)S(1)} %pad_maximum_fusion.2), channel_id=1, source_target_pairs={{16,0},{20,4},{24,8},{28,12},{32,16},{36,20},{40,24},{44,28},{48,3... | collective-permute-start | bytes 1769480 | tf_op jit(solution)/shard_map/ppermute | solution.py:10
  395.8 28.0 %collective-permute-start.5 = (f32[2,1,192,384]{3,2,1,0:T(8,128)S(1)}, f32[2,1,192,384]{3,2,1,0:T(8,128)S(1)}, u32[]{:S(2)}, u32[]{:S(2)}) collective-permute-start(f32[2,1,192,384]{3,2,1,0:T(8,128)S(1)} %pad_maximum_fusion.2), channel_id=1, source_target_pairs={{0,16},{4,20},{8,24},{12,28},{16,32},{20,36},{24,40},{28,44},{32,4... | collective-permute-start | bytes 1769480 | tf_op jit(solution)/shard_map/ppermute | solution.py:10
  538.7 14.8 %collective-permute-start.8 = (f32[2,1,192,384]{3,2,1,0:T(8,128)S(1)}, f32[2,1,192,384]{3,2,1,0:T(8,128)S(1)}, u32[]{:S(2)}, u32[]{:S(2)}) collective-permute-start(f32[2,1,192,384]{3,2,1,0:T(8,128)S(1)} %pad_maximum_fusion.3), channel_id=1, source_target_pairs={{32,0},{36,4},{40,8},{44,12},{48,16},{52,20},{56,24},{60,28},{64,3... | collective-permute-start | bytes 1769480 | tf_op jit(solution)/shard_map/ppermute | solution.py:10
  540.7 14.7 %collective-permute-start.7 = (f32[2,1,192,384]{3,2,1,0:T(8,128)S(1)}, f32[2,1,192,384]{3,2,1,0:T(8,128)S(1)}, u32[]{:S(2)}, u32[]{:S(2)}) collective-permute-start(f32[2,1,192,384]{3,2,1,0:T(8,128)S(1)} %pad_maximum_fusion.3), channel_id=1, source_target_pairs={{0,32},{4,36},{8,40},{12,44},{16,48},{20,52},{24,56},{28,60},{32,6... | collective-permute-start | bytes 1769480 | tf_op jit(solution)/shard_map/ppermute | solution.py:10
  670.3 19.8 %collective-permute-start.10 = (f32[2,1,192,384]{3,2,1,0:T(8,128)S(1)}, f32[2,1,192,384]{3,2,1,0:T(8,128)S(1)}, u32[]{:S(2)}, u32[]{:S(2)}) collective-permute-start(f32[2,1,192,384]{3,2,1,0:T(8,128)S(1)} %pad_maximum_fusion.4), channel_id=1, source_target_pairs={{64,0},{68,4},{72,8},{76,12},{80,16},{84,20},{88,24},{92,28},{96,3... | collective-permute-start | bytes 1769480 | tf_op jit(solution)/shard_map/ppermute | solution.py:10
  671.6 30.1 %collective-permute-start.9 = (f32[2,1,192,384]{3,2,1,0:T(8,128)S(1)}, f32[2,1,192,384]{3,2,1,0:T(8,128)S(1)}, u32[]{:S(2)}, u32[]{:S(2)}) collective-permute-start(f32[2,1,192,384]{3,2,1,0:T(8,128)S(1)} %pad_maximum_fusion.4), channel_id=1, source_target_pairs={{0,64},{4,68},{8,72},{12,76},{16,80},{20,84},{24,88},{28,92},{32,9... | collective-permute-start | bytes 1769480 | tf_op jit(solution)/shard_map/ppermute | solution.py:10
  816.7 32.4 %collective-permute-start.12 = (f32[2,1,192,384]{3,2,1,0:T(8,128)S(1)}, f32[2,1,192,384]{3,2,1,0:T(8,128)S(1)}, u32[]{:S(2)}, u32[]{:S(2)}) collective-permute-start(f32[2,1,192,384]{3,2,1,0:T(8,128)S(1)} %pad_maximum_fusion.5), channel_id=1, source_target_pairs={{128,0},{132,4},{136,8},{140,12},{144,16},{148,20},{152,24},{156,2... | collective-permute-start | bytes 1769480 | tf_op jit(solution)/shard_map/ppermute | solution.py:10
  818.0 31.3 %collective-permute-start.11 = (f32[2,1,192,384]{3,2,1,0:T(8,128)S(1)}, f32[2,1,192,384]{3,2,1,0:T(8,128)S(1)}, u32[]{:S(2)}, u32[]{:S(2)}) collective-permute-start(f32[2,1,192,384]{3,2,1,0:T(8,128)S(1)} %pad_maximum_fusion.5), channel_id=1, source_target_pairs={{0,128},{4,132},{8,136},{12,140},{16,144},{20,148},{24,152},{28,15... | collective-permute-start | bytes 1769480 | tf_op jit(solution)/shard_map/ppermute | solution.py:10
  958.1 2.5 copy-start.2
  997.4 3.5 copy-start
  1003.7 0.9 copy-start.1
Sparse Core Ops, SparseCore 0:
  960.8 36.5 all-gather.2
where the time goes:
time: 1020 us; the launch traced here: 1010 us
  other arithmetic  695 us (68%)
  waiting for transfers between devices  137 us (13%)
  matrix products  80.4 us (8%)
  starting transfers between devices  50.9 us (5%)
  between operations  37.6 us (4%)
  local copies, waits for them, and re-layouts  12.5 us (1%)
    another operation x49, other arithmetic, invert(): imag_factor = jnp.linalg.cholesky(imag_part)  201 us
    another operation x49, other arithmetic, invert(): square_factor = jnp.linalg.cholesky(squared)  201 us
    another operation x28, other arithmetic, invert(): jax.scipy.linalg.cho_solve((square_factor, True), factor_inverse)  141 us
    another operation x30, other arithmetic, invert(): jax.scipy.linalg.solve_triangular(imag_factor, identity, lower=True)  140 us
    ppermute x13, waiting for transfers between devices, shifted(): lax.ppermute(value, axis, [(source, source + steps) for source in range(f...  100 us
    ppermute x13, starting transfers between devices, shifted(): lax.ppermute(value, axis, [(source, source + steps) for source in range(f...  50.8 us
    dot_general x48, matrix products, complex_product(): return jnp.einsum('...ij,...jk->...ik', left, stacked, precision=high)  39.3 us
    all_gather x1, waiting for transfers between devices, shards(): lax.all_gather(green_local[:, None], 'energy', axis=0, tiled=True)[:, 0]  36.6 us
  transfers between devices with their start and end apart: 14, of which 11 were waited for; matrix products, arithmetic and copies ran while one was open for 11% of the time, Pallas kernels for 0%

commit v1 on v0

v1 whole, which is shorter than its diff:
```python
import functools

import jax
import jax.numpy as jnp
from jax import lax
from jax.experimental import pallas as pl
from jax.experimental.pallas import tpu as pltpu
from jax.sharding import PartitionSpec as P

MESH = pl.DeviceIdType.MESH
HALF = 64
TILES = 3
WIDTH = HALF * TILES


def dot(left, right):
    return lax.dot_general(
        left,
        right,
        (((1,), (0,)), ((), ())),
        precision=lax.Precision.HIGH,
        preferred_element_type=jnp.float32,
    )


def lanes_of(rows):
    return lax.broadcasted_iota(jnp.int32, (rows, 128), 1)


def times_i(tile):
    swapped = pltpu.roll(tile, 64, 1)
    return jnp.where(lanes_of(tile.shape[0]) < 64, -swapped, swapped)


def stacked(rows):
    return jnp.concatenate([rows, times_i(rows)], 0)


def row(tile, index):
    return jnp.broadcast_to(tile[index : index + 1, :], tile.shape)


def lane(tile, index):
    return jnp.broadcast_to(tile[:, index : index + 1], tile.shape)


def invert_eight(real, imag, sub):
    real, imag = list(real), list(imag)
    for j in range(8):
        pivot_real, pivot_imag = row(real[j], j), row(imag[j], j)
        scale = 1.0 / (pivot_real * pivot_real + pivot_imag * pivot_imag)
        inv_real, inv_imag = pivot_real * scale, -(pivot_imag * scale)
        own = sub == j
        col_real = real[j] - jnp.where(own, 1.0, 0.0)
        col_imag = imag[j]
        for k in range(8):
            if k == j:
                continue
            row_real, row_imag = row(real[k], j), row(imag[k], j)
            q_real = row_real * inv_real - row_imag * inv_imag
            q_imag = row_real * inv_imag + row_imag * inv_real
            real[k], imag[k] = (
                real[k] - col_real * q_real + col_imag * q_imag,
                imag[k] - col_real * q_imag - col_imag * q_real,
            )
        z_real = jnp.where(own, 1.0, -real[j])
        z_imag = jnp.where(own, 0.0, -imag[j])
        real[j], imag[j] = (
            z_real * inv_real - z_imag * inv_imag,
            z_real * inv_imag + z_imag * inv_real,
        )
    return real, imag


def sweep(panel):
    lanes = lanes_of(8)
    sub = lax.broadcasted_iota(jnp.int32, (8, 128), 0)
    for o in range(0, HALF, 8):
        pivot = panel[o : o + 8]
        real, imag = invert_eight(
            [lane(pivot, o + c) for c in range(8)], [lane(pivot, 64 + o + c) for c in range(8)], sub
        )
        unit = jnp.where(lanes == o + sub, 1.0, 0.0)
        unit_i = jnp.where(lanes == 64 + o + sub, 1.0, 0.0)
        inside = ((lanes >= o) & (lanes < o + 8)) | ((lanes >= 64 + o) & (lanes < 72 + o))
        rows = jnp.where(inside, unit, pivot)
        rows_i = times_i(rows)
        scaled = scaled_i = None
        for c in range(8):
            x, y = row(rows, c), row(rows_i, c)
            a, b = real[c] * x + imag[c] * y, real[c] * y - imag[c] * x
            scaled = a if c == 0 else scaled + a
            scaled_i = b if c == 0 else scaled_i + b
        parts = [jnp.zeros((o, 128), jnp.float32)] if o else []
        parts += [-(scaled + unit), jnp.zeros((56, 128), jnp.float32), -(scaled_i + unit_i)]
        parts += [jnp.zeros((56 - o, 128), jnp.float32)] if o < 56 else []
        after = panel + dot(panel, jnp.concatenate(parts, 0))
        panel = jnp.concatenate(([after[:o]] if o else []) + [scaled, after[o + 8 :]], 0)
    return panel


def invert(block):
    def step(k, carry):
        k1 = lax.rem(k + 1, 3)
        k2 = lax.rem(k + 2, 3)
        own = [pl.ds(pl.multiple_of(t * HALF, HALF), HALF) for t in (k, k1, k2)]
        panel = sweep(jnp.concatenate([block[k, r, :] for r in own], 0))
        rows = jnp.concatenate([stacked(block[k1, own[0], :]), stacked(block[k2, own[0], :])], 1)
        change = dot(panel, rows)
        for i, r in enumerate(own):
            block[k, r, :] = panel[HALF * i : HALF * (i + 1)]
            for j, t in enumerate((k1, k2)):
                part = change[HALF * i : HALF * (i + 1), 128 * j : 128 * (j + 1)]
                block[t, r, :] = part if i == 0 else block[t, r, :] + part
        return carry

    lax.fori_loop(0, 3, step, 0)


def left_of(ref):
    return jnp.concatenate([ref[t] for t in range(TILES)], 1)


def right_tile(tile):
    return jnp.concatenate([stacked(tile[HALF * t : HALF * (t + 1)]) for t in range(TILES)], 0)


def pack(real, imag):
    out = []
    for t in range(TILES):
        out.append(jnp.concatenate([real[:, HALF * t : HALF * (t + 1)], imag[:, HALF * t : HALF * (t + 1)]], 1))
    return out


def store_wide(out, tiles):
    low = lanes_of(WIDTH) < 64
    t0, t1, t2 = tiles
    out[:, 0:128] = jnp.where(low, t0, pltpu.roll(t1, 64, 1))
    out[:, 128:256] = jnp.where(low, t2, t0)
    out[:, 256:384] = jnp.where(low, pltpu.roll(t1, 64, 1), t2)


def load_wide(ref):
    low = lanes_of(WIDTH) < 64
    a, b, c = ref[:, 0:128], ref[:, 128:256], ref[:, 256:384]
    return [
        jnp.where(low, a, b),
        jnp.where(low, pltpu.roll(a, 64, 1), pltpu.roll(c, 64, 1)),
        jnp.where(low, b, c),
    ]


def kernel(
    slabs,
    energies,
    energy_ref,
    broad_ref,
    onsite_ref,
    coupling_ref,
    sigma_ref,
    anharmonic_ref,
    pairs_ref,
    green_ref,
    out_ref,
    below_ref,
    a_ref,
    x_ref,
    lower_ref,
    upper_ref,
    p_ref,
    q_ref,
    p_low,
    q_low,
    p_high,
    q_high,
    all_ref,
    bond_sems,
    send_sems,
    recv_sems,
    gather_sems,
):
    me = lax.axis_index("slab")
    point = lax.axis_index("energy")
    levels = slabs.bit_length() - 1
    barrier = pltpu.get_barrier_semaphore()
    for level in range(levels):
        h = 2**level
        for there, ok in ((me + h, me + h < slabs), (me - h, me >= h)):

            @pl.when(ok)
            def _():
                pl.semaphore_signal(barrier, inc=1, device_id=(there, point), device_id_type=MESH)

    others = [lax.rem(point + d, energies) for d in range(1, energies)]
    for there in others:
        pl.semaphore_signal(barrier, inc=1, device_id=(me, there), device_id_type=MESH)
    peers = energies - 1
    for level in range(levels):
        h = 2**level
        peers = peers + jnp.where(me + h < slabs, 1, 0) + jnp.where(me >= h, 1, 0)
    pl.semaphore_wait(barrier, peers)

    def bond():
        return pltpu.make_async_remote_copy(
            src_ref=coupling_ref,
            dst_ref=below_ref,
            send_sem=bond_sems.at[0],
            recv_sem=bond_sems.at[1],
            device_id=(me + 1, point),
            device_id_type=MESH,
        )

    @pl.when(me + 1 < slabs)
    def _():
        bond().start()

    eye_tiles = []
    for t in range(TILES):
        r = lax.broadcasted_iota(jnp.int32, (WIDTH, HALF), 0)
        c = lax.broadcasted_iota(jnp.int32, (WIDTH, HALF), 1)
        eye_tiles.append(jnp.where(r == c + HALF * t, 1.0, 0.0))
    blank = jnp.zeros((WIDTH, HALF), jnp.float32)
    onsite = onsite_ref[...]
    coupling = coupling_ref[...]
    self_tiles = load_wide(sigma_ref)
    energy = energy_ref[0]
    broad = broad_ref[0]
    for t in range(TILES):
        span = slice(HALF * t, HALF * (t + 1))
        eye = eye_tiles[t]
        a_ref[t] = (
            jnp.concatenate([energy * eye - onsite[:, span], broad * eye], 1) - self_tiles[t]
        )
        upper_ref[t] = jnp.concatenate([-(eye + coupling[:, span]), blank], 1)

    def send(which, kind, tile, level, h):
        src = (p_ref, q_ref, q_ref, p_ref)[kind].at[level, tile]
        dst = (p_low, q_high, q_low, p_high)[kind].at[level, tile]
        there = me + h if kind in (0, 2) else me - h
        return pltpu.make_async_remote_copy(
            src_ref=src,
            dst_ref=dst,
            send_sem=send_sems.at[level, kind, tile],
            recv_sem=recv_sems.at[level, kind, tile],
            device_id=(there, point),
            device_id_type=MESH,
        )

    def times(left, ref, level, sign):
        for t in range(TILES):
            yield t, dot(left, right_tile(ref[level, t]))

    def body(level, h):
        for t in range(TILES):
            x_ref[t] = a_ref[t]
        invert(x_ref)
        before = level - 1
        half = h // 2

        @pl.when(level == 0)
        def _():
            @pl.when(me + 1 < slabs)
            def _():
                bond().wait_send()

            @pl.when(me >= 1)
            def _():
                bond().wait_recv()
                below = below_ref[...].T
                for t in range(TILES):
                    lower_ref[t] = jnp.concatenate(
                        [-(eye_tiles[t] + below[:, HALF * t : HALF * (t + 1)]), blank], 1
                    )

            @pl.when(me < 1)
            def _():
                for t in range(TILES):
                    lower_ref[t] = jnp.zeros((WIDTH, 128), jnp.float32)

        @pl.when((level >= 1) & (level < levels))
        def _():
            @pl.when(me >= half)
            def _():
                left = left_of(lower_ref)
                for t in range(TILES):
                    send(0, 2, t, before, half).wait_recv()
                    lower_ref[t] = -dot(left, right_tile(q_low[before, t]))

            @pl.when(me + half < slabs)
            def _():
                left = left_of(upper_ref)
                for t in range(TILES):
                    send(0, 3, t, before, half).wait_recv()
                    upper_ref[t] = -dot(left, right_tile(p_high[before, t]))

            @pl.when(me + half >= slabs)
            def _():
                for t in range(TILES):
                    upper_ref[t] = jnp.zeros((WIDTH, 128), jnp.float32)

        @pl.when(level < levels)
        def _():
            left = left_of(x_ref)
            up = me + h < slabs
            down = me >= h
            for source, ref, kind, ok in ((upper_ref, p_ref, 0, up), (lower_ref, q_ref, 1, down)):
                for t in range(TILES):
                    ref[level, t] = dot(left, right_tile(source[t]))

                @pl.when(ok)
                def _():
                    for t in range(TILES):
                        send(0, kind, t, level, h).start()

            for kind, other, ref, base, ok in (
                (0, 2, p_low, lower_ref, down),
                (1, 3, q_high, upper_ref, up),
            ):

                @pl.when(ok)
                def _():
                    left = left_of(base)
                    for t in range(TILES):
                        send(0, kind, t, level, h).wait_recv()
                        a_ref[t] = a_ref[t] - dot(left, right_tile(ref[level, t]))

            for kind, other, ok in ((0, 2, up), (1, 3, down)):

                @pl.when(ok)
                def _():
                    for t in range(TILES):
                        send(0, kind, t, level, h).wait_send()

                @pl.when(ok & (level < levels - 1))
                def _():
                    for t in range(TILES):
                        send(0, other, t, level, h).start()

        return h * 2

    lax.fori_loop(0, levels + 1, body, 1)

    def share(d):
        return pltpu.make_async_remote_copy(
            src_ref=x_ref,
            dst_ref=all_ref.at[point],
            send_sem=gather_sems.at[0, d],
            recv_sem=gather_sems.at[1, d],
            device_id=(me, others[d]),
            device_id_type=MESH,
        )

    for d in range(energies - 1):
        share(d).start()
    tiles = [x_ref[t] for t in range(TILES)]
    store_wide(green_ref, tiles)
    for t in range(TILES):
        all_ref[point, t] = tiles[t]
    for d in range(energies - 1):
        share(d).wait()

    def finish(level, h):
        @pl.when(me + h < slabs)
        def _():
            for t in range(TILES):
                send(0, 2, t, level, h).wait_send()

        @pl.when(me >= h)
        def _():
            for t in range(TILES):
                send(0, 3, t, level, h).wait_send()

        return h * 2

    lax.fori_loop(0, levels - 1, finish, 1)

    pairs = pairs_ref.shape[0]
    anharmonic = anharmonic_ref[...] * (1.0 / pairs)
    low = lanes_of(WIDTH) < 64
    outs = []
    for t in range(TILES):
        total = jnp.zeros((WIDTH, 128), jnp.float32)
        for p in range(pairs):
            first = all_ref[pairs_ref[p, 0], t]
            second = all_ref[pairs_ref[p, 1], t]
            flipped = pltpu.roll(second, 64, 1)
            other = pltpu.roll(first, 64, 1)
            total = total + jnp.where(low, first, other) * second + jnp.where(low, -other, first) * flipped
        part = anharmonic[:, HALF * t : HALF * (t + 1)]
        outs.append(total * jnp.concatenate([part, part], 1))
    store_wide(out_ref, outs)


def shards(energy_sq, broadening, onsite, coupling, sigma_in, anharmonic, energy_pairs):
    slabs, energies = lax.axis_size("slab"), lax.axis_size("energy")
    levels = slabs.bit_length() - 1
    block = (TILES, WIDTH, 128)
    vmem = pl.BlockSpec(memory_space=pltpu.VMEM)
    smem = pl.BlockSpec(memory_space=pltpu.SMEM)
    wide = jax.ShapeDtypeStruct((WIDTH, 2 * WIDTH), jnp.float32)
    buffer = pltpu.VMEM(block, jnp.float32)
    stack = pltpu.VMEM((levels,) + block, jnp.float32)
    green, sigma = pl.pallas_call(
        functools.partial(kernel, slabs, energies),
        out_shape=(wide, wide),
        in_specs=[smem, smem, vmem, vmem, vmem, vmem, smem],
        out_specs=(vmem, vmem),
        scratch_shapes=[pltpu.VMEM((WIDTH, WIDTH), jnp.float32)]
        + [buffer] * 4
        + [stack] * 6
        + [pltpu.VMEM((energies,) + block, jnp.float32)]
        + [
            pltpu.SemaphoreType.DMA((2,)),
            pltpu.SemaphoreType.DMA((levels, 4, TILES)),
            pltpu.SemaphoreType.DMA((levels, 4, TILES)),
            pltpu.SemaphoreType.DMA((2, energies - 1)),
        ],
        compiler_params=pltpu.CompilerParams(
            collective_id=0, has_side_effects=True, vmem_limit_bytes=48 * 2**20
        ),
    )(energy_sq, broadening, onsite[0], coupling[0], sigma_in[0, 0], anharmonic[0], energy_pairs[0])
    return green[None, None], sigma[None, None]


def solution(mesh):
    in_specs = (
        P("energy"),
        P("energy"),
        P("slab", None, None),
        P("slab", None, None),
        P("energy", "slab", None, None),
        P("slab", None, None),
        P("energy", None, None),
    )
    out_specs = (P("energy", "slab", None, None), P("energy", "slab", None, None))
    return jax.shard_map(shards, mesh=mesh, in_specs=in_specs, out_specs=out_specs, check_vma=False)
```

time: 1020 us -> 214 us (0.21)
  other arithmetic: 695 us -> 0 us
  Pallas kernels: 0 us -> 206 us
  waiting for transfers between devices: 137 us -> 0 us
  matrix products: 80.4 us -> 0 us
  starting transfers between devices: 50.9 us -> 0 us
  between operations: 37.6 us -> 1.94 us
    another operation x162 -> x0, other arithmetic: 684 us -> none  [the longest x49 201 us: invert(): imag_factor = jnp.linalg.cholesky(imag_part)]
    pallas_call x0 -> x1, Pallas kernels: none -> 206 us  [shards(): pl.pallas_call(functools.partial(kernel, slabs, energies), out_shape=(wid...]
    ppermute x13 -> x0, waiting for transfers between devices: 100 us -> none  [shifted(): lax.ppermute(value, axis, [(source, source + steps) for source in range(f...]
    dot_general x90 -> x0, matrix products: 58.4 us -> none  [the longest x48 39.3 us: complex_product(): return jnp.einsum('...ij,...jk->...ik', left, stacked, precision=high)]
    ppermute x13 -> x0, starting transfers between devices: 50.8 us -> none  [shifted(): lax.ppermute(value, axis, [(source, source + steps) for source in range(f...]
    all_gather x1 -> x0, waiting for transfers between devices: 36.6 us -> none  [shards(): lax.all_gather(green_local[:, None], 'energy', axis=0, tiled=True)[:, 0]]
    another operation x91 -> x0, matrix products: 22 us -> none  [the longest x42 11.4 us: invert(): jax.scipy.linalg.cho_solve((square_factor, True), factor_inverse)]
  transfers between devices with their start and end apart: 14 -> 0, of which waited for: 11 -> 0; matrix products, arithmetic and copies ran while one was open for 11% -> 0% of each run, Pallas kernels for 0% -> 0%
where the time goes in v1:
time: 214 us
  Pallas kernels  206 us (96%)
  local copies, waits for them, and re-layouts  5.92 us (3%)
    pallas_call x1, Pallas kernels, shards(): pl.pallas_call(functools.partial(kernel, slabs, energies), out_shape=(wid...  206 us
    unnamed x12, local copies, waits for them, and re-layouts  5.84 us

profile of v1, /device:TPU:32, one launch (start us, length us, event | category | flops | bytes accessed | tf_op | source)
XLA Modules:
  0.0 213.6 jit_solution(5692453417655816517)
XLA Ops:
  1.9 0.0 copy-start.4
  1.9 0.7 copy-done.4
  2.6 0.1 copy.9.pairs_ref
  2.7 0.0 copy-start
  2.7 1.0 copy-done
  3.6 0.0 copy-start.1
  3.6 0.9 copy-done.1
  4.6 0.0 copy-start.2
  4.6 0.9 copy-done.2
  5.5 0.0 copy-start.3
  5.5 0.9 copy-done.3
  6.4 205.8 %shard_map.86 = (f32[192,384]{1,0:T(8,128)S(1)}, f32[192,384]{1,0:T(8,128)S(1)}) custom-call(f32[1]{0:T(128)S(6)} %copy.12.energy_ref, f32[1]{0:T(128)S(6)} %copy.13.broad_ref, f32[192,192]{1,0:T(8,128)S(1)} %bitcast.10, f32[192,192]{1,0:T(8,128)S(1)} %bitcast.11, f32[192,384]{1,0:T(8,128)S(1)} %bitcast.9, f32[192,192]{1,0:T(8,128)S(1)} %bitcast.12, ...), custom_call_target="tpu_custom_call" | custom-call | tf_op jit(solution)/shard_map/pallas_call | solution.py:403
  212.2 0.7 copy.14
  212.9 0.7 copy.15
Async XLA Ops:
  1.9 0.7 copy-start.4
  2.7 1.0 copy-start
  3.6 0.9 copy-start.1
  4.6 0.9 copy-start.2
  5.5 0.9 copy-start.3

commit v2 on v1

v2 whole, which is shorter than its diff:
```python
import functools

import jax
import jax.numpy as jnp
from jax import lax
from jax.experimental import pallas as pl
from jax.experimental.pallas import tpu as pltpu
from jax.sharding import PartitionSpec as P

MESH = pl.DeviceIdType.MESH
HALF = 64
TILES = 3
WIDTH = HALF * TILES


def dot(left, right, precision=lax.Precision.HIGH):
    return lax.dot_general(
        left,
        right,
        (((1,), (0,)), ((), ())),
        precision=precision,
        preferred_element_type=jnp.float32,
    )


def lanes_of(rows):
    return lax.broadcasted_iota(jnp.int32, (rows, 128), 1)


def times_i(tile):
    swapped = pltpu.roll(tile, 64, 1)
    return jnp.where(lanes_of(tile.shape[0]) < 64, -swapped, swapped)


def stacked(rows):
    return jnp.concatenate([rows, times_i(rows)], 0)


def row(tile, index):
    return jnp.broadcast_to(tile[index : index + 1, :], tile.shape)


def lane(tile, index):
    return jnp.broadcast_to(tile[:, index : index + 1], tile.shape)


def tree(terms):
    terms = list(terms)
    while len(terms) > 1:
        terms = [sum(terms[i + 1 : i + 2], terms[i]) for i in range(0, len(terms), 2)]
    return terms[0]


def eliminate(real, imag, rows, rows_i, sub):
    real, imag = list(real), list(imag)
    for j in range(8):
        pivot_real, pivot_imag = row(real[j], j), row(imag[j], j)
        scale = 1.0 / (pivot_real * pivot_real + pivot_imag * pivot_imag)
        col_real, col_imag = real[j] - jnp.where(sub == j, 1.0, 0.0), imag[j]
        y_real = col_real * pivot_real + col_imag * pivot_imag
        y_imag = col_imag * pivot_real - col_real * pivot_imag
        for k in range(j + 1, 8):
            row_real, row_imag = row(real[k], j), row(imag[k], j)
            real[k], imag[k] = (
                real[k] - (y_real * row_real - y_imag * row_imag) * scale,
                imag[k] - (y_real * row_imag + y_imag * row_real) * scale,
            )
        a, b = row(rows, j), row(rows_i, j)
        rows, rows_i = rows - (y_real * a + y_imag * b) * scale, rows_i - (y_real * b - y_imag * a) * scale
    return rows, rows_i


def sweep(panel):
    lanes = lanes_of(8)
    sub = lax.broadcasted_iota(jnp.int32, (8, 128), 0)
    pivot, following = panel[0:8], panel[8:16]
    for o in range(0, HALF, 8):
        inside = ((lanes >= o) & (lanes < o + 8)) | ((lanes >= 64 + o) & (lanes < 72 + o))

        def less(part, scaled, scaled_i):
            terms = [
                lane(part, o + c) * row(scaled, c) + lane(part, 64 + o + c) * row(scaled_i, c) for c in range(8)
            ]
            return jnp.where(inside, 0.0, part) - tree(terms)

        rows = jnp.where(inside, jnp.where(lanes == o + sub, 1.0, 0.0), pivot)
        scaled, scaled_i = eliminate(
            [lane(pivot, o + c) for c in range(8)],
            [lane(pivot, 64 + o + c) for c in range(8)],
            rows,
            times_i(rows),
            sub,
        )
        known = [scaled]
        if o < HALF - 8:
            pivot = less(following, scaled, scaled_i)
            known.append(pivot)
        if o < HALF - 16:
            following = less(panel[o + 16 : o + 24], scaled, scaled_i)
            known.append(following)
        parts = [jnp.zeros((o, 128), jnp.float32)] if o else []
        parts += [-scaled, jnp.zeros((56, 128), jnp.float32), -scaled_i]
        parts += [jnp.zeros((56 - o, 128), jnp.float32)] if o < 56 else []
        kept = [jnp.where(inside, 0.0, panel[r : r + 8]) for r in range(0, panel.shape[0], 8)]
        after = jnp.concatenate(kept, 0) + dot(panel, jnp.concatenate(parts, 0), lax.Precision.HIGHEST)
        end = o + 8 * len(known)
        panel = jnp.concatenate(([after[:o]] if o else []) + known + ([after[end:]] if end < WIDTH else []), 0)
    return panel


def rows_of(block):
    return pl.ds(pl.multiple_of(block * HALF, HALF), HALF)


def apply(block, panel, order, tile):
    rows = block[tile, rows_of(order[0]), :]
    change = dot(panel, stacked(rows), lax.Precision.HIGHEST)
    for i, r in enumerate(order):
        part = change[HALF * i : HALF * (i + 1)]
        block[tile, rows_of(r), :] = part if i == 0 else block[tile, rows_of(r), :] + part


def invert(block, arrive):
    def step(k, carry):
        arrive(k)
        order = [k, lax.rem(k + 1, 3), lax.rem(k + 2, 3)]

        @pl.when(k == 1)
        def _():
            apply(block, block[0], [0, 1, 2], 1)

        @pl.when(k == 2)
        def _():
            rows = [stacked(block[2, HALF * r : HALF * (r + 1), :]) for r in (0, 1)]
            both = jnp.concatenate([block[0], block[1]], 1)
            change = dot(both, jnp.concatenate(rows, 0), lax.Precision.HIGHEST)
            block[2, 0:128, :] = change[0:128]
            block[2, 128:192, :] = block[2, 128:192, :] + change[128:192]

        panel = sweep(jnp.concatenate([block[k, rows_of(r), :] for r in order], 0))
        for i, r in enumerate(order):
            block[k, rows_of(r), :] = panel[HALF * i : HALF * (i + 1)]

        @pl.when(k >= 1)
        def _():
            apply(block, panel, order, 0)

        @pl.when(k == 2)
        def _():
            apply(block, panel, order, 1)

        return carry

    lax.fori_loop(0, 3, step, 0)


def left_of(ref):
    return jnp.concatenate([ref[t] for t in range(TILES)], 1)


def right_tile(tile):
    return jnp.concatenate([stacked(tile[HALF * t : HALF * (t + 1)]) for t in range(TILES)], 0)


def pack(real, imag):
    out = []
    for t in range(TILES):
        out.append(jnp.concatenate([real[:, HALF * t : HALF * (t + 1)], imag[:, HALF * t : HALF * (t + 1)]], 1))
    return out


def store_wide(out, tiles):
    low = lanes_of(WIDTH) < 64
    t0, t1, t2 = tiles
    out[:, 0:128] = jnp.where(low, t0, pltpu.roll(t1, 64, 1))
    out[:, 128:256] = jnp.where(low, t2, t0)
    out[:, 256:384] = jnp.where(low, pltpu.roll(t1, 64, 1), t2)


def load_wide(ref):
    low = lanes_of(WIDTH) < 64
    a, b, c = ref[:, 0:128], ref[:, 128:256], ref[:, 256:384]
    return [
        jnp.where(low, a, b),
        jnp.where(low, pltpu.roll(a, 64, 1), pltpu.roll(c, 64, 1)),
        jnp.where(low, b, c),
    ]


def kernel(
    slabs,
    energies,
    energy_ref,
    broad_ref,
    onsite_ref,
    coupling_ref,
    sigma_ref,
    anharmonic_ref,
    pairs_ref,
    green_ref,
    out_ref,
    below_ref,
    a_ref,
    x_ref,
    lower_ref,
    upper_ref,
    p_ref,
    q_ref,
    p_low,
    q_low,
    p_high,
    q_high,
    all_0,
    all_1,
    all_2,
    bond_sems,
    send_sems,
    recv_sems,
    gather_sems,
):
    everyone = (all_0, all_1, all_2)
    me = lax.axis_index("slab")
    point = lax.axis_index("energy")
    levels = slabs.bit_length() - 1
    barrier = pltpu.get_barrier_semaphore()
    for level in range(levels):
        h = 2**level
        for there, ok in ((me + h, me + h < slabs), (me - h, me >= h)):

            @pl.when(ok)
            def _():
                pl.semaphore_signal(barrier, inc=1, device_id=(there, point), device_id_type=MESH)

    others = [lax.rem(point + d, energies) for d in range(1, energies)]
    for there in others:
        pl.semaphore_signal(barrier, inc=1, device_id=(me, there), device_id_type=MESH)
    peers = energies - 1
    for level in range(levels):
        h = 2**level
        peers = peers + jnp.where(me + h < slabs, 1, 0) + jnp.where(me >= h, 1, 0)
    pl.semaphore_wait(barrier, peers)

    def bond():
        return pltpu.make_async_remote_copy(
            src_ref=coupling_ref,
            dst_ref=below_ref,
            send_sem=bond_sems.at[0],
            recv_sem=bond_sems.at[1],
            device_id=(me + 1, point),
            device_id_type=MESH,
        )

    @pl.when(me + 1 < slabs)
    def _():
        bond().start()

    eye_tiles = []
    for t in range(TILES):
        r = lax.broadcasted_iota(jnp.int32, (WIDTH, HALF), 0)
        c = lax.broadcasted_iota(jnp.int32, (WIDTH, HALF), 1)
        eye_tiles.append(jnp.where(r == c + HALF * t, 1.0, 0.0))
    blank = jnp.zeros((WIDTH, HALF), jnp.float32)
    onsite = onsite_ref[...]
    coupling = coupling_ref[...]
    self_tiles = load_wide(sigma_ref)
    energy = energy_ref[0]
    broad = broad_ref[0]
    for t in range(TILES):
        span = slice(HALF * t, HALF * (t + 1))
        eye = eye_tiles[t]
        a_ref[t] = (
            jnp.concatenate([energy * eye - onsite[:, span], broad * eye], 1) - self_tiles[t]
        )
        upper_ref[t] = jnp.concatenate([-(eye + coupling[:, span]), blank], 1)

    def clear(level, h):
        for t in range(TILES):

            @pl.when(me < h)
            def _():
                p_low[level, t] = jnp.zeros((WIDTH, 128), jnp.float32)
                q_low[level, t] = jnp.zeros((WIDTH, 128), jnp.float32)

            @pl.when(me + h >= slabs)
            def _():
                p_high[level, t] = jnp.zeros((WIDTH, 128), jnp.float32)
                q_high[level, t] = jnp.zeros((WIDTH, 128), jnp.float32)

        return h * 2

    lax.fori_loop(0, levels, clear, 1)

    def send(kind, tile, level, h):
        src = (p_ref, q_ref, q_ref, p_ref)[kind].at[level, tile]
        dst = (p_low, q_high, q_low, p_high)[kind].at[level, tile]
        there = me + h if kind in (0, 2) else me - h
        return pltpu.make_async_remote_copy(
            src_ref=src,
            dst_ref=dst,
            send_sem=send_sems.at[level, kind, tile],
            recv_sem=recv_sems.at[level, kind, tile],
            device_id=(there, point),
            device_id_type=MESH,
        )

    def body(level, h):
        before = level - 1
        half = h // 2
        low_before = (level >= 1) & (me >= half)
        high_before = (level >= 1) & (me + half < slabs)

        def arrive(k):
            @pl.when(low_before)
            def _():
                send(0, k, before, half).wait_recv()

            @pl.when(high_before)
            def _():
                send(1, k, before, half).wait_recv()

            @pl.when(level >= 1)
            def _():
                left = jnp.concatenate([left_of(lower_ref), left_of(upper_ref)], 1)
                right = jnp.concatenate([right_tile(p_low[before, k]), right_tile(q_high[before, k])], 0)
                a_ref[k] = a_ref[k] - dot(left, right)

            x_ref[k] = a_ref[k]

        invert(x_ref, arrive)

        @pl.when(level == 0)
        def _():
            @pl.when(me + 1 < slabs)
            def _():
                bond().wait_send()

            @pl.when(me >= 1)
            def _():
                bond().wait_recv()
                below = below_ref[...].T
                for t in range(TILES):
                    lower_ref[t] = jnp.concatenate(
                        [-(eye_tiles[t] + below[:, HALF * t : HALF * (t + 1)]), blank], 1
                    )

            @pl.when(me < 1)
            def _():
                for t in range(TILES):
                    lower_ref[t] = jnp.zeros((WIDTH, 128), jnp.float32)

        @pl.when(low_before & (level < levels))
        def _():
            for t in range(TILES):
                send(2, t, before, half).wait_recv()

        @pl.when(high_before & (level < levels))
        def _():
            for t in range(TILES):
                send(3, t, before, half).wait_recv()

        @pl.when((level >= 1) & (level < levels))
        def _():
            left = left_of(lower_ref)
            for t in range(TILES):
                lower_ref[t] = -dot(left, right_tile(q_low[before, t]))
            left = left_of(upper_ref)
            for t in range(TILES):
                upper_ref[t] = -dot(left, right_tile(p_high[before, t]))

        @pl.when(level < levels)
        def _():
            left = left_of(x_ref)
            up = me + h < slabs
            down = me >= h
            for t in range(TILES):
                both = dot(left, jnp.concatenate([right_tile(upper_ref[t]), right_tile(lower_ref[t])], 1))
                p_ref[level, t] = both[:, :128]
                q_ref[level, t] = both[:, 128:]

                @pl.when(up)
                def _():
                    send(0, t, level, h).start()

                @pl.when(down)
                def _():
                    send(1, t, level, h).start()

            for t in range(TILES):

                @pl.when(up & (level < levels - 1))
                def _():
                    send(2, t, level, h).start()

                @pl.when(down & (level < levels - 1))
                def _():
                    send(3, t, level, h).start()

        return h * 2

    lax.fori_loop(0, levels + 1, body, 1)

    def share(d, t):
        return pltpu.make_async_remote_copy(
            src_ref=x_ref.at[t],
            dst_ref=everyone[t].at[point],
            send_sem=gather_sems.at[0, d, t],
            recv_sem=gather_sems.at[1, d, t],
            device_id=(me, others[d]),
            device_id_type=MESH,
        )

    for t in range(TILES):
        for d in range(energies - 1):
            share(d, t).start()
    tiles = [x_ref[t] for t in range(TILES)]
    store_wide(green_ref, tiles)
    for t in range(TILES):
        everyone[t][point] = tiles[t]

    def finish(level, h):
        for t in range(TILES):
            for kind, ok in ((0, me + h < slabs), (1, me >= h)):

                @pl.when(ok)
                def _():
                    send(kind, t, level, h).wait_send()

                @pl.when(ok & (level < levels - 1))
                def _():
                    send(kind + 2, t, level, h).wait_send()

        return h * 2

    lax.fori_loop(0, levels, finish, 1)

    pairs = pairs_ref.shape[0]
    anharmonic = anharmonic_ref[...] * (1.0 / pairs)
    low = lanes_of(WIDTH) < 64
    outs = []
    for t in range(TILES):
        for d in range(energies - 1):
            share(d, t).wait()
        total = jnp.zeros((WIDTH, 128), jnp.float32)
        for p in range(pairs):
            first = everyone[t][pairs_ref[p, 0]]
            second = everyone[t][pairs_ref[p, 1]]
            flipped = pltpu.roll(second, 64, 1)
            other = pltpu.roll(first, 64, 1)
            total = total + jnp.where(low, first, other) * second + jnp.where(low, -other, first) * flipped
        part = anharmonic[:, HALF * t : HALF * (t + 1)]
        outs.append(total * jnp.concatenate([part, part], 1))
    store_wide(out_ref, outs)


def shards(energy_sq, broadening, onsite, coupling, sigma_in, anharmonic, energy_pairs):
    slabs, energies = lax.axis_size("slab"), lax.axis_size("energy")
    levels = slabs.bit_length() - 1
    block = (TILES, WIDTH, 128)
    vmem = pl.BlockSpec(memory_space=pltpu.VMEM)
    smem = pl.BlockSpec(memory_space=pltpu.SMEM)
    wide = jax.ShapeDtypeStruct((WIDTH, 2 * WIDTH), jnp.float32)
    buffer = pltpu.VMEM(block, jnp.float32)
    stack = pltpu.VMEM((levels,) + block, jnp.float32)
    green, sigma = pl.pallas_call(
        functools.partial(kernel, slabs, energies),
        out_shape=(wide, wide),
        in_specs=[smem, smem, vmem, vmem, vmem, vmem, smem],
        out_specs=(vmem, vmem),
        scratch_shapes=[pltpu.VMEM((WIDTH, WIDTH), jnp.float32)]
        + [buffer] * 4
        + [stack] * 6
        + [pltpu.VMEM((energies, WIDTH, 128), jnp.float32)] * TILES
        + [
            pltpu.SemaphoreType.DMA((2,)),
            pltpu.SemaphoreType.DMA((levels, 4, TILES)),
            pltpu.SemaphoreType.DMA((levels, 4, TILES)),
            pltpu.SemaphoreType.DMA((2, energies - 1, TILES)),
        ],
        compiler_params=pltpu.CompilerParams(
            collective_id=0, has_side_effects=True, vmem_limit_bytes=48 * 2**20
        ),
    )(energy_sq, broadening, onsite[0], coupling[0], sigma_in[0, 0], anharmonic[0], energy_pairs[0])
    return green[None, None], sigma[None, None]


def solution(mesh):
    in_specs = (
        P("energy"),
        P("energy"),
        P("slab", None, None),
        P("slab", None, None),
        P("energy", "slab", None, None),
        P("slab", None, None),
        P("energy", None, None),
    )
    out_specs = (P("energy", "slab", None, None), P("energy", "slab", None, None))
    return jax.shard_map(shards, mesh=mesh, in_specs=in_specs, out_specs=out_specs, check_vma=False)
```

time: 214 us -> 170 us (0.79)
  Pallas kernels: 206 us -> 162 us
    pallas_call x1, Pallas kernels: 206 us -> 162 us  [shards(): pl.pallas_call(functools.partial(kernel, slabs, energies), out_shape=(wid...]
where the time goes in v2:
time: 170 us; the launch traced here: 169 us
  Pallas kernels  162 us (95%)
  local copies, waits for them, and re-layouts  5.92 us (3%)
  between operations  1.94 us (1%)
    pallas_call x1, Pallas kernels, shards(): pl.pallas_call(functools.partial(kernel, slabs, energies), out_shape=(wid...  162 us
    unnamed x12, local copies, waits for them, and re-layouts  5.84 us

profile of v2, /device:TPU:32, one launch (start us, length us, event | category | flops | bytes accessed | tf_op | source)
XLA Modules:
  0.0 169.4 jit_solution(8858296316442561233)
XLA Ops:
  1.9 0.0 copy-start.4
  1.9 0.7 copy-done.4
  2.6 0.1 copy.9.pairs_ref
  2.7 0.0 copy-start
  2.7 1.0 copy-done
  3.6 0.0 copy-start.1
  3.6 0.9 copy-done.1
  4.6 0.0 copy-start.2
  4.6 0.9 copy-done.2
  5.5 0.0 copy-start.3
  5.5 0.9 copy-done.3
  6.4 161.6 %shard_map.86 = (f32[192,384]{1,0:T(8,128)S(1)}, f32[192,384]{1,0:T(8,128)S(1)}) custom-call(f32[1]{0:T(128)S(6)} %copy.12.energy_ref, f32[1]{0:T(128)S(6)} %copy.13.broad_ref, f32[192,192]{1,0:T(8,128)S(1)} %bitcast.10, f32[192,192]{1,0:T(8,128)S(1)} %bitcast.11, f32[192,384]{1,0:T(8,128)S(1)} %bitcast.9, f32[192,192]{1,0:T(8,128)S(1)} %bitcast.12, ...), custom_call_target="tpu_custom_call" | custom-call | tf_op jit(solution)/shard_map/pallas_call | solution.py:464
  168.0 0.7 copy.14
  168.7 0.7 copy.15
Async XLA Ops:
  1.9 0.7 copy-start.4
  2.7 1.0 copy-start
  3.6 0.9 copy-start.1
  4.6 0.9 copy-start.2
  5.5 0.9 copy-start.3

commit v3 on v2

--- a/solution.py
+++ b/solution.py
@@ -21,6 +21,23 @@
         precision=precision,
         preferred_element_type=jnp.float32,
     )
+
+
+def split(value):
+    high = value.astype(jnp.bfloat16)
+    return high, (value - high.astype(jnp.float32)).astype(jnp.bfloat16)
+
+
+def dot16(left, right):
+    return lax.dot_general(left, right, (((1,), (0,)), ((), ())), preferred_element_type=jnp.float32)
+
+
+def product(left, right):
+    left_high, left_low = left
+    right_high, right_low = split(right)
+    width = right.shape[1]
+    both = dot16(left_high, jnp.concatenate([right_high, right_low], 1))
+    return both[:, :width] + (both[:, width:] + dot16(left_low, right_high))
 
 
 def lanes_of(rows):
@@ -114,7 +131,7 @@
 
 def apply(block, panel, order, tile):
     rows = block[tile, rows_of(order[0]), :]
-    change = dot(panel, stacked(rows), lax.Precision.HIGHEST)
+    change = product(split(panel), stacked(rows))
     for i, r in enumerate(order):
         part = change[HALF * i : HALF * (i + 1)]
         block[tile, rows_of(r), :] = part if i == 0 else block[tile, rows_of(r), :] + part
@@ -133,7 +150,7 @@
         def _():
             rows = [stacked(block[2, HALF * r : HALF * (r + 1), :]) for r in (0, 1)]
             both = jnp.concatenate([block[0], block[1]], 1)
-            change = dot(both, jnp.concatenate(rows, 0), lax.Precision.HIGHEST)
+            change = product(split(both), jnp.concatenate(rows, 0))
             block[2, 0:128, :] = change[0:128]
             block[2, 128:192, :] = block[2, 128:192, :] + change[128:192]
 
@@ -202,8 +219,10 @@
     below_ref,
     a_ref,
     x_ref,
-    lower_ref,
-    upper_ref,
+    high_ref,
+    low_ref,
+    x_high,
+    x_low,
     p_ref,
     q_ref,
     p_low,
@@ -240,6 +259,10 @@
         peers = peers + jnp.where(me + h < slabs, 1, 0) + jnp.where(me >= h, 1, 0)
     pl.semaphore_wait(barrier, peers)
 
+    @pl.when(me < 1)
+    def _():
+        below_ref[...] = jnp.zeros((WIDTH, WIDTH), jnp.float32)
+
     def bond():
         return pltpu.make_async_remote_copy(
             src_ref=coupling_ref,
@@ -260,8 +283,8 @@
         c = lax.broadcasted_iota(jnp.int32, (WIDTH, HALF), 1)
         eye_tiles.append(jnp.where(r == c + HALF * t, 1.0, 0.0))
     blank = jnp.zeros((WIDTH, HALF), jnp.float32)
+    eye_whole = jnp.concatenate(eye_tiles, 1)
     onsite = onsite_ref[...]
-    coupling = coupling_ref[...]
     self_tiles = load_wide(sigma_ref)
     energy = energy_ref[0]
     broad = broad_ref[0]
@@ -271,7 +294,6 @@
         a_ref[t] = (
             jnp.concatenate([energy * eye - onsite[:, span], broad * eye], 1) - self_tiles[t]
         )
-        upper_ref[t] = jnp.concatenate([-(eye + coupling[:, span]), blank], 1)
 
     def clear(level, h):
         for t in range(TILES):
@@ -320,13 +342,39 @@
 
             @pl.when(level >= 1)
             def _():
-                left = jnp.concatenate([left_of(lower_ref), left_of(upper_ref)], 1)
+                left = high_ref[lax.rem(before, 2)], low_ref[lax.rem(before, 2)]
                 right = jnp.concatenate([right_tile(p_low[before, k]), right_tile(q_high[before, k])], 0)
-                a_ref[k] = a_ref[k] - dot(left, right)
+                a_ref[k] = a_ref[k] - product(left, right)
 
             x_ref[k] = a_ref[k]
 
         invert(x_ref, arrive)
+        for t in range(TILES):
+            high, low = split(x_ref[t])
+            x_high[:, 128 * t : 128 * (t + 1)] = high
+            x_low[:, 128 * t : 128 * (t + 1)] = low
+
+        up = me + h < slabs
+        down = me >= h
+        now = lax.rem(level, 2)
+        then = 1 - now
+
+        def keep(t, lower, upper):
+            for base, tile in ((0, lower), (384, upper)):
+                high, low = split(tile)
+                high_ref[now, :, base + 128 * t : base + 128 * (t + 1)] = high
+                low_ref[now, :, base + 128 * t : base + 128 * (t + 1)] = low
+            both = product((x_high[...], x_low[...]), jnp.concatenate([right_tile(upper), right_tile(lower)], 1))
+            p_ref[level, t] = both[:, :128]
+            q_ref[level, t] = both[:, 128:]
+
+            @pl.when(up)
+            def _():
+                send(0, t, level, h).start()
+
+            @pl.when(down)
+            def _():
+                send(1, t, level, h).start()
 
         @pl.when(level == 0)
         def _():
@@ -337,63 +385,43 @@
             @pl.when(me >= 1)
             def _():
                 bond().wait_recv()
-                below = below_ref[...].T
-                for t in range(TILES):
-                    lower_ref[t] = jnp.concatenate(
-                        [-(eye_tiles[t] + below[:, HALF * t : HALF * (t + 1)]), blank], 1
-                    )
-
-            @pl.when(me < 1)
-            def _():
-                for t in range(TILES):
-                    lower_ref[t] = jnp.zeros((WIDTH, 128), jnp.float32)
-
-        @pl.when(low_before & (level < levels))
+
+            below = jnp.where(me > 0, eye_whole + below_ref[...].T, 0.0)
+            for t in range(TILES):
+                span = slice(HALF * t, HALF * (t + 1))
+                keep(
+                    t,
+                    jnp.concatenate([-below[:, span], blank], 1),
+                    jnp.concatenate([-(eye_tiles[t] + coupling_ref[:, span]), blank], 1),
+                )
+
+        @pl.when((level >= 1) & (level < levels))
         def _():
             for t in range(TILES):
-                send(2, t, before, half).wait_recv()
-
-        @pl.when(high_before & (level < levels))
-        def _():
-            for t in range(TILES):
-                send(3, t, before, half).wait_recv()
-
-        @pl.when((level >= 1) & (level < levels))
-        def _():
-            left = left_of(lower_ref)
-            for t in range(TILES):
-                lower_ref[t] = -dot(left, right_tile(q_low[before, t]))
-            left = left_of(upper_ref)
-            for t in range(TILES):
-                upper_ref[t] = -dot(left, right_tile(p_high[before, t]))
-
-        @pl.when(level < levels)
-        def _():
-            left = left_of(x_ref)
-            up = me + h < slabs
-            down = me >= h
-            for t in range(TILES):
-                both = dot(left, jnp.concatenate([right_tile(upper_ref[t]), right_tile(lower_ref[t])], 1))
-                p_ref[level, t] = both[:, :128]
-                q_ref[level, t] = both[:, 128:]
-
-                @pl.when(up)
+
+                @pl.when(low_before)
                 def _():
-                    send(0, t, level, h).start()
-
-                @pl.when(down)
+                    send(2, t, before, half).wait_recv()
+
+                @pl.when(high_before)
                 def _():
-                    send(1, t, level, h).start()
-
-            for t in range(TILES):
-
-                @pl.when(up & (level < levels - 1))
-                def _():
-                    send(2, t, level, h).start()
-
-                @pl.when(down & (level < levels - 1))
-                def _():
-                    send(3, t, level, h).start()
+                    send(3, t, before, half).wait_recv()
+
+                keep(
+                    t,
+                    -product((high_ref[then, :, 0:384], low_ref[then, :, 0:384]), right_tile(q_low[before, t])),
+                    -product((high_ref[then, :, 384:768], low_ref[then, :, 384:768]), right_tile(p_high[before, t])),
+                )
+
+        for t in range(TILES):
+
+            @pl.when(up & (level < levels - 1))
+            def _():
+                send(2, t, level, h).start()
+
+            @pl.when(down & (level < levels - 1))
+            def _():
+                send(3, t, level, h).start()
 
         return h * 2
 
@@ -467,7 +495,9 @@
         in_specs=[smem, smem, vmem, vmem, vmem, vmem, smem],
         out_specs=(vmem, vmem),
         scratch_shapes=[pltpu.VMEM((WIDTH, WIDTH), jnp.float32)]
-        + [buffer] * 4
+        + [buffer] * 2
+        + [pltpu.VMEM((2, WIDTH, 4 * WIDTH), jnp.bfloat16)] * 2
+        + [pltpu.VMEM((WIDTH, 2 * WIDTH), jnp.bfloat16)] * 2
         + [stack] * 6
         + [pltpu.VMEM((energies, WIDTH, 128), jnp.float32)] * TILES
         + [

time: 170 us -> 166 us (0.976)
  Pallas kernels: 162 us -> 158 us
    pallas_call x1, Pallas kernels: 162 us -> 158 us  [shards(): pl.pallas_call(functools.partial(kernel, slabs, energies), out_shape=(wid...]
where the time goes in v3:
time: 166 us
  Pallas kernels  158 us (95%)
  local copies, waits for them, and re-layouts  5.92 us (4%)
  between operations  1.94 us (1%)
    pallas_call x1, Pallas kernels, shards(): pl.pallas_call(functools.partial(kernel, slabs, energies), out_shape=(wid...  158 us
    unnamed x12, local copies, waits for them, and re-layouts  5.84 us

profile of v3, /device:TPU:32, one launch (start us, length us, event | category | flops | bytes accessed | tf_op | source)
XLA Modules:
  0.0 166.0 jit_solution(2083960392694740180)
XLA Ops:
  1.9 0.0 copy-start.4
  1.9 0.7 copy-done.4
  2.6 0.1 copy.9.pairs_ref
  2.7 0.0 copy-start
  2.7 1.0 copy-done
  3.6 0.0 copy-start.1
  3.6 0.9 copy-done.1
  4.6 0.0 copy-start.2
  4.6 0.9 copy-done.2
  5.5 0.0 copy-start.3
  5.5 0.9 copy-done.3
  6.4 158.1 %shard_map.86 = (f32[192,384]{1,0:T(8,128)S(1)}, f32[192,384]{1,0:T(8,128)S(1)}) custom-call(f32[1]{0:T(128)S(6)} %copy.12.energy_ref, f32[1]{0:T(128)S(6)} %copy.13.broad_ref, f32[192,192]{1,0:T(8,128)S(1)} %bitcast.10, f32[192,192]{1,0:T(8,128)S(1)} %bitcast.11, f32[192,384]{1,0:T(8,128)S(1)} %bitcast.9, f32[192,192]{1,0:T(8,128)S(1)} %bitcast.12, ...), custom_call_target="tpu_custom_call" | custom-call | tf_op jit(solution)/shard_map/pallas_call | solution.py:492
  164.5 0.7 copy.14
  165.3 0.7 copy.15
Async XLA Ops:
  1.9 0.7 copy-start.4
  2.7 1.0 copy-start
  3.6 0.9 copy-start.1
  4.6 0.9 copy-start.2
  5.5 0.9 copy-start.3

commit v4 on v3

--- a/solution.py
+++ b/solution.py
@@ -209,13 +209,18 @@
     energies,
     energy_ref,
     broad_ref,
+    onsite_arg,
+    coupling_arg,
+    sigma_arg,
+    anharmonic_arg,
+    pairs_ref,
+    green_ref,
+    out_ref,
     onsite_ref,
     coupling_ref,
     sigma_ref,
     anharmonic_ref,
-    pairs_ref,
-    green_ref,
-    out_ref,
+    load_sems,
     below_ref,
     a_ref,
     x_ref,
@@ -232,6 +237,7 @@
     all_0,
     all_1,
     all_2,
+    turned,
     bond_sems,
     send_sems,
     recv_sems,
@@ -241,6 +247,19 @@
     me = lax.axis_index("slab")
     point = lax.axis_index("energy")
     levels = slabs.bit_length() - 1
+    loads = [
+        pltpu.make_async_copy(source, target, load_sems.at[i])
+        for i, (source, target) in enumerate(
+            (
+                (coupling_arg, coupling_ref),
+                (sigma_arg, sigma_ref),
+                (onsite_arg, onsite_ref),
+                (anharmonic_arg, anharmonic_ref),
+            )
+        )
+    ]
+    for load in loads:
+        load.start()
     barrier = pltpu.get_barrier_semaphore()
     for level in range(levels):
         h = 2**level
@@ -253,12 +272,6 @@
     others = [lax.rem(point + d, energies) for d in range(1, energies)]
     for there in others:
         pl.semaphore_signal(barrier, inc=1, device_id=(me, there), device_id_type=MESH)
-    peers = energies - 1
-    for level in range(levels):
-        h = 2**level
-        peers = peers + jnp.where(me + h < slabs, 1, 0) + jnp.where(me >= h, 1, 0)
-    pl.semaphore_wait(barrier, peers)
-
     @pl.when(me < 1)
     def _():
         below_ref[...] = jnp.zeros((WIDTH, WIDTH), jnp.float32)
@@ -273,10 +286,6 @@
             device_id_type=MESH,
         )
 
-    @pl.when(me + 1 < slabs)
-    def _():
-        bond().start()
-
     eye_tiles = []
     for t in range(TILES):
         r = lax.broadcasted_iota(jnp.int32, (WIDTH, HALF), 0)
@@ -284,6 +293,8 @@
         eye_tiles.append(jnp.where(r == c + HALF * t, 1.0, 0.0))
     blank = jnp.zeros((WIDTH, HALF), jnp.float32)
     eye_whole = jnp.concatenate(eye_tiles, 1)
+    for load in loads[:3]:
+        load.wait()
     onsite = onsite_ref[...]
     self_tiles = load_wide(sigma_ref)
     energy = energy_ref[0]
@@ -294,6 +305,16 @@
         a_ref[t] = (
             jnp.concatenate([energy * eye - onsite[:, span], broad * eye], 1) - self_tiles[t]
         )
+
+    peers = energies - 1
+    for level in range(levels):
+        h = 2**level
+        peers = peers + jnp.where(me + h < slabs, 1, 0) + jnp.where(me >= h, 1, 0)
+    pl.semaphore_wait(barrier, peers)
+
+    @pl.when(me + 1 < slabs)
+    def _():
+        bond().start()
 
     def clear(level, h):
         for t in range(TILES):
@@ -364,10 +385,14 @@
                 high, low = split(tile)
                 high_ref[now, :, base + 128 * t : base + 128 * (t + 1)] = high
                 low_ref[now, :, base + 128 * t : base + 128 * (t + 1)] = low
-            both = product((x_high[...], x_low[...]), jnp.concatenate([right_tile(upper), right_tile(lower)], 1))
+            return jnp.concatenate([right_tile(upper), right_tile(lower)], 1)
+
+        def spread(t, couplings):
+            both = product((x_high[...], x_low[...]), couplings)
             p_ref[level, t] = both[:, :128]
             q_ref[level, t] = both[:, 128:]
 
+        def pass_on(t):
             @pl.when(up)
             def _():
                 send(0, t, level, h).start()
@@ -375,6 +400,14 @@
             @pl.when(down)
             def _():
                 send(1, t, level, h).start()
+
+        def couple(t):
+            old = high_ref[then], low_ref[then]
+            return keep(
+                t,
+                -product((old[0][:, 0:384], old[1][:, 0:384]), right_tile(q_low[before, t])),
+                -product((old[0][:, 384:768], old[1][:, 384:768]), right_tile(p_high[before, t])),
+            )
 
         @pl.when(level == 0)
         def _():
@@ -389,14 +422,19 @@
             below = jnp.where(me > 0, eye_whole + below_ref[...].T, 0.0)
             for t in range(TILES):
                 span = slice(HALF * t, HALF * (t + 1))
-                keep(
+                spread(
                     t,
-                    jnp.concatenate([-below[:, span], blank], 1),
-                    jnp.concatenate([-(eye_tiles[t] + coupling_ref[:, span]), blank], 1),
+                    keep(
+                        t,
+                        jnp.concatenate([-below[:, span], blank], 1),
+                        jnp.concatenate([-(eye_tiles[t] + coupling_ref[:, span]), blank], 1),
+                    ),
                 )
+                pass_on(t)
 
         @pl.when((level >= 1) & (level < levels))
         def _():
+            couplings = None
             for t in range(TILES):
 
                 @pl.when(low_before)
@@ -407,11 +445,14 @@
                 def _():
                     send(3, t, before, half).wait_recv()
 
-                keep(
-                    t,
-                    -product((high_ref[then, :, 0:384], low_ref[then, :, 0:384]), right_tile(q_low[before, t])),
-                    -product((high_ref[then, :, 384:768], low_ref[then, :, 384:768]), right_tile(p_high[before, t])),
-                )
+                after = couple(t)
+                if t:
+                    spread(t - 1, couplings)
+                    pass_on(t - 1)
+                couplings = after
+
+            spread(TILES - 1, couplings)
+            pass_on(TILES - 1)
 
         for t in range(TILES):
 
@@ -461,6 +502,7 @@
 
     lax.fori_loop(0, levels, finish, 1)
 
+    loads[3].wait()
     pairs = pairs_ref.shape[0]
     anharmonic = anharmonic_ref[...] * (1.0 / pairs)
     low = lanes_of(WIDTH) < 64
@@ -468,13 +510,14 @@
     for t in range(TILES):
         for d in range(energies - 1):
             share(d, t).wait()
-        total = jnp.zeros((WIDTH, 128), jnp.float32)
+        for e in range(energies):
+            turned[t, e] = pltpu.roll(everyone[t][e], 64, 1)
+        straight = crossed = jnp.zeros((WIDTH, 128), jnp.float32)
         for p in range(pairs):
             first = everyone[t][pairs_ref[p, 0]]
-            second = everyone[t][pairs_ref[p, 1]]
-            flipped = pltpu.roll(second, 64, 1)
-            other = pltpu.roll(first, 64, 1)
-            total = total + jnp.where(low, first, other) * second + jnp.where(low, -other, first) * flipped
+            straight = straight + first * everyone[t][pairs_ref[p, 1]]
+            crossed = crossed + first * turned[t, pairs_ref[p, 1]]
+        total = jnp.where(low, straight - pltpu.roll(straight, 64, 1), crossed + pltpu.roll(crossed, 64, 1))
         part = anharmonic[:, HALF * t : HALF * (t + 1)]
         outs.append(total * jnp.concatenate([part, part], 1))
     store_wide(out_ref, outs)
@@ -486,20 +529,24 @@
     block = (TILES, WIDTH, 128)
     vmem = pl.BlockSpec(memory_space=pltpu.VMEM)
     smem = pl.BlockSpec(memory_space=pltpu.SMEM)
+    hbm = pl.BlockSpec(memory_space=pltpu.HBM)
+    square = pltpu.VMEM((WIDTH, WIDTH), jnp.float32)
     wide = jax.ShapeDtypeStruct((WIDTH, 2 * WIDTH), jnp.float32)
     buffer = pltpu.VMEM(block, jnp.float32)
     stack = pltpu.VMEM((levels,) + block, jnp.float32)
     green, sigma = pl.pallas_call(
         functools.partial(kernel, slabs, energies),
         out_shape=(wide, wide),
-        in_specs=[smem, smem, vmem, vmem, vmem, vmem, smem],
+        in_specs=[smem, smem, hbm, hbm, hbm, hbm, smem],
         out_specs=(vmem, vmem),
-        scratch_shapes=[pltpu.VMEM((WIDTH, WIDTH), jnp.float32)]
+        scratch_shapes=[square, square, pltpu.VMEM((WIDTH, 2 * WIDTH), jnp.float32), square]
+        + [pltpu.SemaphoreType.DMA((4,)), square]
         + [buffer] * 2
         + [pltpu.VMEM((2, WIDTH, 4 * WIDTH), jnp.bfloat16)] * 2
         + [pltpu.VMEM((WIDTH, 2 * WIDTH), jnp.bfloat16)] * 2
         + [stack] * 6
         + [pltpu.VMEM((energies, WIDTH, 128), jnp.float32)] * TILES
+        + [pltpu.VMEM((TILES, energies, WIDTH, 128), jnp.float32)]
         + [
             pltpu.SemaphoreType.DMA((2,)),
             pltpu.SemaphoreType.DMA((levels, 4, TILES)),
@@ -507,7 +554,7 @@
             pltpu.SemaphoreType.DMA((2, energies - 1, TILES)),
         ],
         compiler_params=pltpu.CompilerParams(
-            collective_id=0, has_side_effects=True, vmem_limit_bytes=48 * 2**20
+            collective_id=0, has_side_effects=True, vmem_limit_bytes=58 * 2**20
         ),
     )(energy_sq, broadening, onsite[0], coupling[0], sigma_in[0, 0], anharmonic[0], energy_pairs[0])
     return green[None, None], sigma[None, None]

time: 166 us -> 165 us (level)
  local copies, waits for them, and re-layouts: 5.92 us -> 3.8 us
    unnamed x12 -> x6, local copies, waits for them, and re-layouts: 5.84 us -> 3.13 us
where the time goes in v4:
time: 165 us; the launch traced here: 164 us
  Pallas kernels  158 us (96%)
  local copies, waits for them, and re-layouts  3.8 us (2%)
  between operations  1.95 us (1%)
    pallas_call x1, Pallas kernels, shards(): pl.pallas_call(functools.partial(kernel, slabs, energies), out_shape=(wid...  158 us

profile of v4, /device:TPU:32, one launch (start us, length us, event | category | flops | bytes accessed | tf_op | source)
XLA Modules:
  0.0 163.9 jit_solution(8424567360517933527)
XLA Ops:
  1.9 0.0 copy-start.1
  1.9 0.7 copy-done.1
  2.6 0.7 copy.9.pairs_ref
  3.3 158.1 %shard_map.86 = (f32[192,384]{1,0:T(8,128)}, f32[192,384]{1,0:T(8,128)}) custom-call(f32[1]{0:T(128)S(6)} %copy.12.energy_ref, f32[1]{0:T(128)S(6)} %copy.13.broad_ref, f32[192,192]{1,0:T(8,128)} %bitcast.10, f32[192,192]{1,0:T(8,128)} %bitcast.11, f32[192,384]{1,0:T(8,128)} %bitcast.9, f32[192,192]{1,0:T(8,128)} %bitcast.12, s32[8,2]{1,0:T(8,128)} %copy.9.pairs_ref), custom_call_target="tpu_custom_call" | custom-call | tf_op jit(solution)/shard_map/pallas_call | solution.py:537
  161.4 0.0 copy-start
  161.4 1.7 %copy.14 = f32[1,1,192,384]{3,2,1,0:T(8,128)} copy(f32[1,1,192,384]{3,2,1,0:T(8,128)} %bitcast.8) | data formatting | bytes 589824
  163.1 0.0 copy-done
  163.1 0.7 copy.15
Async XLA Ops:
  1.9 0.7 copy-start.1
  161.4 1.8 %copy-start = (f32[192,384]{1,0:T(8,128)S(1)}, f32[192,384]{1,0:T(8,128)}, u32[]{:S(2)}) copy-start(f32[192,384]{1,0:T(8,128)} %get-tuple-element.5) | copy-start | bytes 884740
